TPU v7x, 256 devices: a whole 4x4x8 slice. The times are simulated.
256 devices in a mesh: batch: 8 (over x, core), slab: 32 (over y, z).
Axes of the slice: x: 4, y: 4, z: 8, core: 2. Of those that a mesh axis runs over, the one named last changes fastest.
Arguments:
- volume: bfloat16 [8, 32, 128, 16, 128], P('batch', None, 'slab'), may hold values from -6 to 6
- kernel: bfloat16 [32, 32, 3, 3, 3], replicated, may hold values from -0.21875 to 0.21875
- offset: float32 [32], replicated, may hold values from -1 to 1
- upstream: bfloat16 [8, 32, 128, 16, 128], P('batch', None, 'slab'), may hold values from -6 to 6
Outputs:
- activated: bfloat16 [8, 32, 128, 16, 128], P('batch', None, 'slab')
- grad_volume: bfloat16 [8, 32, 128, 16, 128], P('batch', None, 'slab')
- grad_kernel: float32 [32, 32, 3, 3, 3], replicated
- grad_offset: float32 [32], replicated
All inputs are finite; a program needn't handle non-finite values.
Results may differ from a plain program's by a relative error of at most 0.0085.
Values may be sent and summed in bfloat16 or wider, within the bound.
A program may use at most 64 MiB of HBM per device.

v0:
```python
import jax
import jax.numpy as jnp
from jax import lax
from jax.sharding import PartitionSpec as P


def padded_2(block, sides, width):
    for axis, dim in sides:
        count = lax.axis_size(axis)
        forward = [(i, i + 1) for i in range(count - 1)]
        backward = [(target, source) for source, target in forward]
        low = lax.ppermute(
            lax.slice_in_dim(block, block.shape[dim] - width, None, axis=dim), axis, forward
        )
        high = lax.ppermute(lax.slice_in_dim(block, 0, width, axis=dim), axis, backward)
        block = jnp.concatenate([low, block, high], axis=dim)
    return block


def convolve_depth(field, weights):
    return lax.conv_general_dilated(
        field,
        weights,
        (1, 1, 1),
        ((0, 0), (1, 1), (1, 1)),
        dimension_numbers=("NCDHW", "OIDHW", "NCDHW"),
        preferred_element_type=jnp.float32,
    )


def pre_gradient(preact, cotangent):
    sig = jax.nn.sigmoid(preact)
    output = (preact * sig).astype(jnp.bfloat16)
    grad_pre = (cotangent.astype(jnp.float32) * sig * (1.0 + preact * (1.0 - sig))).astype(
        jnp.bfloat16
    )
    return (output, grad_pre)


def kernel_terms(haloed, grad_pre, planes):
    rows, cols = (grad_pre.shape[3], grad_pre.shape[4])
    padded = jnp.pad(haloed, ((0, 0), (0, 0), (0, 0), (1, 1), (1, 1)))
    terms = []
    for first in range(3):
        for second in range(3):
            for third in range(3):
                window = padded[
                    :, :, first : first + planes, second : second + rows, third : third + cols
                ]
                terms.append(
                    jnp.einsum(
                        "nodhw,nidhw->oi", grad_pre, window, preferred_element_type=jnp.float32
                    )
                )
    return jnp.stack(terms, axis=2)


def on_device(volume, kernel, offset, upstream):
    planes = volume.shape[2]
    flipped = jnp.transpose(jnp.flip(kernel, (2, 3, 4)), (1, 0, 2, 3, 4))
    bias = offset[None, :, None, None, None]
    haloed = padded_2(volume, (("slab", 2),), 1)
    preact = convolve_depth(haloed, kernel) + bias
    activated, grad_pre = pre_gradient(preact, upstream)
    grad_haloed = padded_2(grad_pre, (("slab", 2),), 1)
    grad_volume = convolve_depth(grad_haloed, flipped).astype(jnp.bfloat16)
    local_kernel = kernel_terms(haloed, grad_pre, planes).reshape(kernel.shape)
    local_offset = jnp.sum(grad_pre.astype(jnp.float32), axis=(0, 2, 3, 4))
    summed_kernel, summed_offset = lax.psum((local_kernel, local_offset), ("batch", "slab"))
    cells = (
        volume.shape[0]
        * planes
        * volume.shape[3]
        * volume.shape[4]
        * lax.axis_size("batch")
        * lax.axis_size("slab")
    )
    scale = 1.0 / jnp.sqrt(jnp.float32(cells))
    return (activated, grad_volume, summed_kernel * scale, summed_offset * scale)


def solution(mesh):
    placed = (P("batch", None, "slab", None, None), P(), P(), P("batch", None, "slab", None, None))
    return jax.shard_map(
        on_device,
        mesh=mesh,
        in_specs=placed,
        out_specs=(
            P("batch", None, "slab", None, None),
            P("batch", None, "slab", None, None),
            P(),
            P(),
        ),
        check_vma=False,
    )
```

profile of v0, /device:TPU:1, one launch (start us, length us, event | category | flops | bytes accessed | tf_op | source)
XLA Modules:
  0.0 333.9 jit_solution(11143610916050945041)
XLA Ops:
  7.2 1.4 copy.135
  8.7 4.4 %collective-permute-start = (bf16[1,32,1,16,128]{4,1,3,2,0:T(8,128)(2,1)S(1)}, bf16[1,32,1,16,128]{4,1,3,2,0:T(8,128)(2,1)S(1)}, u32[]{:S(2)}, u32[]{:S(2)}) collective-permute-start(bf16[1,32,1,16,128]{4,1,3,2,0:T(8,128)(2,1)S(1)} %get-tuple-element.24), channel_id=1, source_target_pairs={{0,1},{1,2},{2,3},{3,4},{4,5},{5,6},{6,7},{7,8},{8,9},{9,10},{10,1... | collective-permute-start | bytes 393224 | tf_op jit(solution)/shard_map/ppermute | solution.py:12
  13.1 1.3 collective-permute-start.1
  14.4 3.2 copy.142
  17.6 1.5 constant_dynamic-update-slice_fusion.1
  19.4 3.4 %copy.207 = bf16[32,6,16,1,128]{0,2,4,1,3:T(8,128)(2,1)} copy(bf16[32,6,16,1,128]{4,0,2,1,3:T(8,128)(2,1)S(1)} %bitcast.363) | data formatting | bytes 1572864
  22.8 2.5 pad.5.clone
  25.4 0.9 copy.140
  26.4 8.8 %add_divide_fusion = (f32[4,16,8,17,32]{4,2,3,1,0:T(8,128)S(1)}, bf16[4,16,8,17,32]{4,2,3,1,0:T(8,128)(2,1)S(1)}, f32[4,16,8,17,32]{4,2,3,1,0:T(8,128)S(1)}) fusion(f32[32]{0:T(128)S(1)} %copy-done.10, pred[8,17]{0,1:T(8,128)(4,1)S(1)} %copy-done.11, bf16[32,32,3,3,3]{1,0,4,3,2:T(8,128)(2,1)S(1)} %copy-done, bf16[32,6,16,1,7,2]{0,4,5,2,1,3:T(8,128)(2,1)S(1)} %slice.134, ...), kind=kOutput, calls=%fused_computation.30 | convolution fusion | flops 466829312 | bytes 3762440 | tf_op jit(solution)/shard_map/conv_general_dilated | solution.py:21
  35.3 0.4 copy.141
  35.6 1.7 slice_bitcast_fusion.3
  37.3 0.8 copy.144
  38.1 1.0 copy.143
  39.1 1.3 convert_reduce_fusion
  40.6 1.1 copy-done.1
  41.7 2.8 copy.148
  45.2 0.4 fusion.47
  45.6 0.4 fusion.46
  46.2 0.4 fusion.44
  46.6 0.4 fusion.43
  47.2 0.4 fusion.41
  47.6 0.4 fusion.40
  48.2 0.4 fusion.38
  48.6 0.4 fusion.37
  49.0 0.5 fusion.36
  49.4 0.4 fusion.35
  49.8 0.4 fusion.34
  50.4 0.4 fusion.32
  50.8 0.4 fusion.31
  51.4 0.4 fusion.29
  51.8 0.4 fusion.28
  52.4 0.4 fusion.26
  53.4 0.4 fusion.23
  53.8 0.8 copy-done.5
  54.6 81.2 %psum.15 = f32[32]{0:T(128)S(1)} all-reduce(f32[32]{0:T(128)S(1)} %get-tuple-element.16), channel_id=1, replica_groups=mesh['batch'=8,'slab'=32] {'batch','slab'}, use_global_device_ids=true, to_apply=%region_2.3 | all-reduce | flops 32 | bytes 256 | tf_op jit(solution)/shard_map/psum | solution.py:69
  135.8 0.5 broadcast_multiply_fusion.1
  136.3 4.0 %copy.178 = bf16[1,32,4,16,128]{4,3,2,1,0:T(8,128)(2,1)} copy(bf16[1,32,4,16,128]{1,3,4,2,0:T(8,128)(2,1)} %slice_bitcast_fusion.3) | data formatting | bytes 1048576
  140.3 1.3 collective-permute-start.3
  141.6 4.3 %collective-permute-start.2 = (bf16[1,32,1,16,128]{1,3,4,2,0:T(8,128)(2,1)S(1)}, bf16[1,32,1,16,128]{1,3,4,2,0:T(8,128)(2,1)S(1)}, u32[]{:S(2)}, u32[]{:S(2)}) collective-permute-start(bf16[1,32,1,16,128]{1,3,4,2,0:T(8,128)(2,1)S(1)} %get-tuple-element.21), channel_id=1, source_target_pairs={{0,1},{1,2},{2,3},{3,4},{4,5},{5,6},{6,7},{7,8},{8,9},{9,10},{10,1... | collective-permute-start | bytes 393224 | tf_op jit(solution)/shard_map/ppermute | solution.py:12
  145.8 164.6 %all-reduce.3.cloned.1.call-done = f32[32,32,3,3,3]{1,0,4,3,2:T(8,128)} async-done(((f32[32,32,3,3,3]{1,0,4,3,2:T(8,128)}), f32[32,32,3,3,3]{1,0,4,3,2:T(8,128)}) %all-reduce.3.cloned.1.call-update) | async-done | bytes 110608 | tf_op jit(solution)/shard_map/psum | solution.py:69
  310.4 1.8 broadcast_multiply_fusion
  312.3 2.3 maximum_bitcast_fusion
  314.6 0.6 pad.7
  315.2 0.9 copy.146
  316.2 7.2 %select_convert_fusion = bf16[4,16,8,17,32]{4,2,3,1,0:T(8,128)(2,1)S(1)} fusion(pred[8,17]{0,1:T(8,128)(4,1)S(1)} %copy-done.11, bf16[32,32,3,3,3]{1,0,4,3,2:T(8,128)(2,1)S(1)} %copy-done, bf16[32,6,16,1,7,2]{0,4,5,2,1,3:T(8,128)(2,1)S(1)} %slice.140, bf16[32,6,16,1,8,17]{0,4,5,2,1,3:T(8,128)(2,1)S(1)} %copy.146), kind=kOutput, calls=%fused_computation.27 | convolution fusion | flops 464601088 | bytes 1534088 | tf_op jit(solution)/shard_map/conv_general_dilated | solution.py:21
  323.4 0.4 copy.147
  323.8 0.4 slice_bitcast_fusion.2
  324.2 2.9 copy.179
  (44 shorter events, 3.8 us)
Async XLA Ops:
  7.2 19.2 %copy-start = (bf16[32,32,3,3,3]{1,0,4,3,2:T(8,128)(2,1)S(1)}, bf16[32,32,3,3,3]{1,0,4,3,2:T(8,128)(2,1)}, u32[]{:S(2)}) copy-start(bf16[32,32,3,3,3]{1,0,4,3,2:T(8,128)(2,1)} %param.5) | copy-start | bytes 165892
  7.2 303.3 %all-reduce.3.cloned.1.call-start = ((), (), s32[]{:S(2)}) async-start(), calls=%async_computation | async-start | bytes 884736 | tf_op jit(solution)/shard_map/psum | solution.py:69
  8.7 8.9 %copy-start.3 = (bf16[1,32,4,16,128]{4,1,3,2,0:T(8,128)(2,1)}, bf16[1,32,4,16,128]{4,1,3,2,0:T(8,128)(2,1)S(1)}, u32[]{:S(2)}) copy-start(bf16[1,32,4,16,128]{4,1,3,2,0:T(8,128)(2,1)S(1)} %copy.135) | copy-start | bytes 1572868
  8.7 8.9 %collective-permute-start = (bf16[1,32,1,16,128]{4,1,3,2,0:T(8,128)(2,1)S(1)}, bf16[1,32,1,16,128]{4,1,3,2,0:T(8,128)(2,1)S(1)}, u32[]{:S(2)}, u32[]{:S(2)}) collective-permute-start(bf16[1,32,1,16,128]{4,1,3,2,0:T(8,128)(2,1)S(1)} %get-tuple-element.24), channel_id=1, source_target_pairs={{0,1},{1,2},{2,3},{3,4},{4,5},{5,6},{6,7},{7,8},{8,9},{9,10},{10,1... | collective-permute-start | bytes 393224 | tf_op jit(solution)/shard_map/ppermute | solution.py:12
  13.1 6.3 %collective-permute-start.1 = (bf16[1,32,1,16,128]{4,1,3,2,0:T(8,128)(2,1)S(1)}, bf16[1,32,1,16,128]{4,1,3,2,0:T(8,128)(2,1)S(1)}, u32[]{:S(2)}, u32[]{:S(2)}) collective-permute-start(bf16[1,32,1,16,128]{4,1,3,2,0:T(8,128)(2,1)S(1)} %get-tuple-element.23), channel_id=1, source_target_pairs={{1,0},{2,1},{3,2},{4,3},{5,4},{6,5},{7,6},{8,7},{9,8},{10,9},{11,1... | collective-permute-start | bytes 393224 | tf_op jit(solution)/shard_map/ppermute | solution.py:15
  17.6 7.7 %copy-start.8 = (bf16[1,32,1,16,128]{4,1,3,2,0:T(8,128)(2,1)}, bf16[1,32,1,16,128]{4,1,3,2,0:T(8,128)(2,1)S(1)}, u32[]{:S(2)}) copy-start(bf16[1,32,1,16,128]{4,1,3,2,0:T(8,128)(2,1)S(1)} %collective-permute-done) | copy-start | bytes 393220
  19.4 6.0 %copy-start.6 = (bf16[1,32,1,16,128]{4,1,3,2,0:T(8,128)(2,1)}, bf16[1,32,1,16,128]{4,1,3,2,0:T(8,128)(2,1)S(1)}, u32[]{:S(2)}) copy-start(bf16[1,32,1,16,128]{4,1,3,2,0:T(8,128)(2,1)S(1)} %collective-permute-done.1) | copy-start | bytes 393220
  25.4 1.0 copy-start.10
  25.4 1.0 copy-start.11
  40.4 1.3 copy-start.1
  41.7 4.2 %copy-start.4 = (bf16[1,32,4,16,128]{4,1,3,2,0:T(8,128)(2,1)S(1)}, bf16[1,32,4,16,128]{4,1,3,2,0:T(8,128)(2,1)}, u32[]{:S(2)}) copy-start(bf16[1,32,4,16,128]{4,1,3,2,0:T(8,128)(2,1)} %copy-done.3) | copy-start | bytes 1572868
  44.5 1.4 copy-start.9
  47.2 1.7 copy-start.2
  50.4 1.7 copy-start.7
  53.8 0.8 copy-start.5
  140.3 172.0 %collective-permute-start.3 = (bf16[1,32,1,16,128]{1,3,4,2,0:T(8,128)(2,1)S(1)}, bf16[1,32,1,16,128]{1,3,4,2,0:T(8,128)(2,1)S(1)}, u32[]{:S(2)}, u32[]{:S(2)}) collective-permute-start(bf16[1,32,1,16,128]{1,3,4,2,0:T(8,128)(2,1)S(1)} %get-tuple-element.22), channel_id=1, source_target_pairs={{1,0},{2,1},{3,2},{4,3},{5,4},{6,5},{7,6},{8,7},{9,8},{10,9},{11,1... | collective-permute-start | bytes 393224 | tf_op jit(solution)/shard_map/ppermute | solution.py:15
  141.6 170.7 %collective-permute-start.2 = (bf16[1,32,1,16,128]{1,3,4,2,0:T(8,128)(2,1)S(1)}, bf16[1,32,1,16,128]{1,3,4,2,0:T(8,128)(2,1)S(1)}, u32[]{:S(2)}, u32[]{:S(2)}) collective-permute-start(bf16[1,32,1,16,128]{1,3,4,2,0:T(8,128)(2,1)S(1)} %get-tuple-element.21), channel_id=1, source_target_pairs={{0,1},{1,2},{2,3},{3,4},{4,5},{5,6},{6,7},{7,8},{8,9},{9,10},{10,1... | collective-permute-start | bytes 393224 | tf_op jit(solution)/shard_map/ppermute | solution.py:12
Sparse Core Ops, SparseCore 0:
  54.7 255.6 all-reduce.2
where the time goes:
time: 334 us
  waiting for transfers between devices  165 us (49%)
  blocking collectives  81.2 us (24%)
  local copies, waits for them, and re-layouts  31 us (9%)
  matrix products  25.2 us (8%)
  between operations  14.4 us (4%)
  starting transfers between devices  11.3 us (3%)
  other arithmetic  5.9 us (2%)
    psum x1, waiting for transfers between devices, on_device(): lax.psum((local_kernel, local_offset), ('batch', 'slab'))  165 us
    psum x1, blocking collectives, on_device(): lax.psum((local_kernel, local_offset), ('batch', 'slab'))  81.2 us
    unnamed x31, local copies, waits for them, and re-layouts  18.4 us
    conv_general_dilated x2, matrix products, convolve_depth(): lax.conv_general_dilated(field, weights, (1, 1, 1), ((0, 0), (1, 1), (1,...  16.1 us
    dot_general x27, matrix products, kernel_terms(): jnp.einsum('nodhw,nidhw->oi', grad_pre, window, preferred_element_type=jn...  9.17 us
    ppermute x2, starting transfers between devices, padded_2(): lax.ppermute(lax.slice_in_dim(block, block.shape[dim] - width, None, axis...  8.66 us
  transfers between devices with their start and end apart: 5, of which 2 were waited for; matrix products, arithmetic and copies ran while one was open for 3% of the time, Pallas kernels for 0%

commit v1 on v0

--- a/solution.py
+++ b/solution.py
@@ -66,7 +66,7 @@
     grad_volume = convolve_depth(grad_haloed, flipped).astype(jnp.bfloat16)
     local_kernel = kernel_terms(haloed, grad_pre, planes).reshape(kernel.shape)
     local_offset = jnp.sum(grad_pre.astype(jnp.float32), axis=(0, 2, 3, 4))
-    summed_kernel, summed_offset = lax.psum((local_kernel, local_offset), ("batch", "slab"))
+    summed_kernel, summed_offset = lax.psum(lax.psum((local_kernel, local_offset), "batch"), "slab")
     cells = (
         volume.shape[0]
         * planes

time: 334 us -> 302 us (0.904); the launches traced: 334 us -> 298 us
  waiting for transfers between devices: 165 us -> 135 us
  blocking collectives: 81.2 us -> 75.4 us
    psum x1 -> x2, waiting for transfers between devices: 165 us -> 134 us  [the longest x1 134 us: on_device(): lax.psum(lax.psum((local_kernel, local_offset), 'batch'), 'slab')]
    psum x1 -> x2, blocking collectives: 81.2 us -> 75.4 us  [the longest x1 61.9 us: on_device(): lax.psum(lax.psum((local_kernel, local_offset), 'batch'), 'slab')]
  transfers between devices with their start and end apart: 5 -> 6, of which waited for: 2 -> 2; matrix products, arithmetic and copies ran while one was open for 3% -> 12% of each run, Pallas kernels for 0% -> 0%
where the time goes in v1:
time: 302 us; the launch traced here: 298 us
  waiting for transfers between devices  135 us (45%)
  blocking collectives  75.4 us (25%)
  local copies, waits for them, and re-layouts  31 us (10%)
  matrix products  25.2 us (8%)
  between operations  14.4 us (5%)
  starting transfers between devices  11.6 us (4%)
  other arithmetic  5.82 us (2%)
    psum x1, waiting for transfers between devices, on_device(): lax.psum(lax.psum((local_kernel, local_offset), 'batch'), 'slab')  134 us
    psum x1, blocking collectives, on_device(): lax.psum(lax.psum((local_kernel, local_offset), 'batch'), 'slab')  61.9 us
    unnamed x31, local copies, waits for them, and re-layouts  17.2 us
    conv_general_dilated x2, matrix products, convolve_depth(): lax.conv_general_dilated(field, weights, (1, 1, 1), ((0, 0), (1, 1), (1,...  16.1 us
    psum x1, blocking collectives, on_device(): lax.psum((local_kernel, local_offset), 'batch')  13.5 us
    dot_general x27, matrix products, kernel_terms(): jnp.einsum('nodhw,nidhw->oi', grad_pre, window, preferred_element_type=jn...  9.18 us
    ppermute x2, starting transfers between devices, padded_2(): lax.ppermute(lax.slice_in_dim(block, block.shape[dim] - width, None, axis...  8.92 us
  transfers between devices with their start and end apart: 6, of which 2 were waited for; matrix products, arithmetic and copies ran while one was open for 12% of the time, Pallas kernels for 0%

profile of v1, /device:TPU:1, one launch (start us, length us, event | category | flops | bytes accessed | tf_op | source)
XLA Modules:
  0.0 298.1 jit_solution(12646396375612248914)
XLA Ops:
  7.2 1.4 copy.135
  8.7 4.4 %collective-permute-start = (bf16[1,32,1,16,128]{4,1,3,2,0:T(8,128)(2,1)S(1)}, bf16[1,32,1,16,128]{4,1,3,2,0:T(8,128)(2,1)S(1)}, u32[]{:S(2)}, u32[]{:S(2)}) collective-permute-start(bf16[1,32,1,16,128]{4,1,3,2,0:T(8,128)(2,1)S(1)} %get-tuple-element.24), channel_id=1, source_target_pairs={{0,1},{1,2},{2,3},{3,4},{4,5},{5,6},{6,7},{7,8},{8,9},{9,10},{10,1... | collective-permute-start | bytes 393224 | tf_op jit(solution)/shard_map/ppermute | solution.py:12
  13.1 1.3 collective-permute-start.1
  14.4 3.2 %copy.142 = bf16[1,32,4,16,128]{1,3,4,2,0:T(8,128)(2,1)S(1)} copy(bf16[1,32,4,16,128]{4,3,2,1,0:T(8,128)(2,1)} %param.7) | data formatting | bytes 1048576 | tf_op args[3]
  17.6 1.5 constant_dynamic-update-slice_fusion.1
  19.4 3.4 %copy.207 = bf16[32,6,16,1,128]{0,2,4,1,3:T(8,128)(2,1)} copy(bf16[32,6,16,1,128]{4,0,2,1,3:T(8,128)(2,1)S(1)} %bitcast.363) | data formatting | bytes 1572864
  22.9 2.5 pad.5.clone
  25.4 0.9 copy.140
  26.4 8.8 %add_divide_fusion = (f32[4,16,8,17,32]{4,2,3,1,0:T(8,128)S(1)}, bf16[4,16,8,17,32]{4,2,3,1,0:T(8,128)(2,1)S(1)}, f32[4,16,8,17,32]{4,2,3,1,0:T(8,128)S(1)}) fusion(f32[32]{0:T(128)S(1)} %copy-done.10, pred[8,17]{0,1:T(8,128)(4,1)S(1)} %copy-done.11, bf16[32,32,3,3,3]{1,0,4,3,2:T(8,128)(2,1)S(1)} %copy-done, bf16[32,6,16,1,7,2]{0,4,5,2,1,3:T(8,128)(2,1)S(1)} %slice.134, ...), kind=kOutput, calls=%fused_computation.30 | convolution fusion | flops 466829312 | bytes 3762440 | tf_op jit(solution)/shard_map/conv_general_dilated | solution.py:21
  35.3 0.4 copy.141
  35.6 1.7 slice_bitcast_fusion.3
  37.3 0.8 copy.144
  38.1 1.0 copy.143
  39.1 1.2 convert_reduce_fusion
  40.3 1.3 fusion.138
  41.6 1.3 collective-permute-start.3
  42.9 4.5 %collective-permute-start.2 = (bf16[1,32,1,16,128]{1,3,4,2,0:T(8,128)(2,1)}, bf16[1,32,1,16,128]{1,3,4,2,0:T(8,128)(2,1)S(1)}, u32[]{:S(2)}, u32[]{:S(2)}) collective-permute-start(bf16[1,32,1,16,128]{1,3,4,2,0:T(8,128)(2,1)} %get-tuple-element.21), channel_id=1, source_target_pairs={{0,1},{1,2},{2,3},{3,4},{4,5},{5,6},{6,7},{7,8},{8,9},{9,10},{10,1... | collective-permute-start | bytes 393224 | tf_op jit(solution)/shard_map/ppermute | solution.py:12
  47.5 2.8 copy.148
  50.9 0.4 fusion.47
  51.3 0.4 fusion.46
  52.0 0.4 fusion.44
  53.0 0.4 fusion.41
  53.3 0.4 fusion.40
  54.0 0.4 fusion.38
  54.3 0.4 fusion.37
  54.7 0.5 fusion.36
  55.2 0.4 fusion.35
  55.5 0.4 fusion.34
  56.2 0.4 fusion.32
  56.5 0.4 fusion.31
  57.2 0.4 fusion.29
  57.5 0.4 fusion.28
  58.2 0.4 fusion.26
  59.2 0.4 fusion.23
  59.6 0.8 copy-done.5
  60.4 13.5 %psum.30 = f32[32]{0:T(128)S(1)} all-reduce(f32[32]{0:T(128)S(1)} %get-tuple-element.16), channel_id=1, replica_groups=mesh['batch'=8,'slab'=32] {'batch'}, use_global_device_ids=true, to_apply=%region_3.4 | all-reduce | flops 32 | bytes 256 | tf_op jit(solution)/shard_map/psum | solution.py:69
  73.9 61.9 %psum.31 = f32[32]{0:T(128)S(1)} all-reduce(f32[32]{0:T(128)S(1)} %psum.30), channel_id=1, replica_groups=mesh['batch'=8,'slab'=32] {'slab'}, use_global_device_ids=true, to_apply=%region_4.5 | all-reduce | flops 32 | bytes 256 | tf_op jit(solution)/shard_map/psum | solution.py:69
  135.8 0.5 broadcast_multiply_fusion.1
  136.3 4.0 %copy.178 = bf16[1,32,4,16,128]{4,3,2,1,0:T(8,128)(2,1)} copy(bf16[1,32,4,16,128]{1,3,4,2,0:T(8,128)(2,1)} %slice_bitcast_fusion.3) | data formatting | bytes 1048576
  140.3 2.3 maximum_bitcast_fusion
  142.7 0.6 pad.7
  143.3 0.9 copy.146
  144.3 7.2 %select_convert_fusion = bf16[4,16,8,17,32]{4,2,3,1,0:T(8,128)(2,1)S(1)} fusion(pred[8,17]{0,1:T(8,128)(4,1)S(1)} %copy-done.11, bf16[32,32,3,3,3]{1,0,4,3,2:T(8,128)(2,1)S(1)} %copy-done, bf16[32,6,16,1,7,2]{0,4,5,2,1,3:T(8,128)(2,1)S(1)} %slice.140, bf16[32,6,16,1,8,17]{0,4,5,2,1,3:T(8,128)(2,1)S(1)} %copy.146), kind=kOutput, calls=%fused_computation.27 | convolution fusion | flops 464601088 | bytes 1534088 | tf_op jit(solution)/shard_map/conv_general_dilated | solution.py:21
  151.5 0.4 copy.147
  151.9 0.4 slice_bitcast_fusion.2
  152.2 2.9 copy.179
  155.1 134.3 %all-reduce.6.cloned.1.call-done = f32[32,32,3,3,3]{1,0,4,3,2:T(8,128)} async-done(((f32[32,32,3,3,3]{1,0,4,3,2:T(8,128)}), f32[32,32,3,3,3]{1,0,4,3,2:T(8,128)}) %all-reduce.6.cloned.1.call-update) | async-done | bytes 110608 | tf_op jit(solution)/shard_map/psum | solution.py:69
  289.4 1.8 broadcast_multiply_fusion
  (48 shorter events, 4.0 us)
Async XLA Ops:
  7.2 19.2 %copy-start = (bf16[32,32,3,3,3]{1,0,4,3,2:T(8,128)(2,1)S(1)}, bf16[32,32,3,3,3]{1,0,4,3,2:T(8,128)(2,1)}, u32[]{:S(2)}) copy-start(bf16[32,32,3,3,3]{1,0,4,3,2:T(8,128)(2,1)} %param.5) | copy-start | bytes 165892
  7.2 133.1 %all-reduce.4.cloned.1.call-start = ((), (), s32[]{:S(2)}) async-start(), calls=%async_computation | async-start | bytes 884736 | tf_op jit(solution)/shard_map/psum | solution.py:69
  8.7 8.9 %copy-start.3 = (bf16[1,32,4,16,128]{4,1,3,2,0:T(8,128)(2,1)}, bf16[1,32,4,16,128]{4,1,3,2,0:T(8,128)(2,1)S(1)}, u32[]{:S(2)}) copy-start(bf16[1,32,4,16,128]{4,1,3,2,0:T(8,128)(2,1)S(1)} %copy.135) | copy-start | bytes 1572868
  8.7 8.9 %collective-permute-start = (bf16[1,32,1,16,128]{4,1,3,2,0:T(8,128)(2,1)S(1)}, bf16[1,32,1,16,128]{4,1,3,2,0:T(8,128)(2,1)S(1)}, u32[]{:S(2)}, u32[]{:S(2)}) collective-permute-start(bf16[1,32,1,16,128]{4,1,3,2,0:T(8,128)(2,1)S(1)} %get-tuple-element.24), channel_id=1, source_target_pairs={{0,1},{1,2},{2,3},{3,4},{4,5},{5,6},{6,7},{7,8},{8,9},{9,10},{10,1... | collective-permute-start | bytes 393224 | tf_op jit(solution)/shard_map/ppermute | solution.py:12
  13.1 6.3 %collective-permute-start.1 = (bf16[1,32,1,16,128]{4,1,3,2,0:T(8,128)(2,1)S(1)}, bf16[1,32,1,16,128]{4,1,3,2,0:T(8,128)(2,1)S(1)}, u32[]{:S(2)}, u32[]{:S(2)}) collective-permute-start(bf16[1,32,1,16,128]{4,1,3,2,0:T(8,128)(2,1)S(1)} %get-tuple-element.23), channel_id=1, source_target_pairs={{1,0},{2,1},{3,2},{4,3},{5,4},{6,5},{7,6},{8,7},{9,8},{10,9},{11,1... | collective-permute-start | bytes 393224 | tf_op jit(solution)/shard_map/ppermute | solution.py:15
  17.6 7.8 %copy-start.8 = (bf16[1,32,1,16,128]{4,1,3,2,0:T(8,128)(2,1)}, bf16[1,32,1,16,128]{4,1,3,2,0:T(8,128)(2,1)S(1)}, u32[]{:S(2)}) copy-start(bf16[1,32,1,16,128]{4,1,3,2,0:T(8,128)(2,1)S(1)} %collective-permute-done) | copy-start | bytes 393220
  19.4 6.0 %copy-start.6 = (bf16[1,32,1,16,128]{4,1,3,2,0:T(8,128)(2,1)}, bf16[1,32,1,16,128]{4,1,3,2,0:T(8,128)(2,1)S(1)}, u32[]{:S(2)}) copy-start(bf16[1,32,1,16,128]{4,1,3,2,0:T(8,128)(2,1)S(1)} %collective-permute-done.1) | copy-start | bytes 393220
  25.4 1.0 copy-start.10
  25.4 1.0 copy-start.11
  40.3 7.1 %copy-start.1 = (bf16[1,32,4,16,128]{1,3,4,2,0:T(8,128)(2,1)}, bf16[1,32,4,16,128]{1,3,4,2,0:T(8,128)(2,1)S(1)}, u32[]{:S(2)}) copy-start(bf16[1,32,4,16,128]{1,3,4,2,0:T(8,128)(2,1)S(1)} %get-tuple-element.17) | copy-start | bytes 1572868
  41.6 98.7 %collective-permute-start.3 = (bf16[1,32,1,16,128]{1,3,4,2,0:T(8,128)(2,1)}, bf16[1,32,1,16,128]{1,3,4,2,0:T(8,128)(2,1)S(1)}, u32[]{:S(2)}, u32[]{:S(2)}) collective-permute-start(bf16[1,32,1,16,128]{1,3,4,2,0:T(8,128)(2,1)} %get-tuple-element.22), channel_id=1, source_target_pairs={{1,0},{2,1},{3,2},{4,3},{5,4},{6,5},{7,6},{8,7},{9,8},{10,9},{11,1... | collective-permute-start | bytes 393224 | tf_op jit(solution)/shard_map/ppermute | solution.py:15
  42.9 97.4 %collective-permute-start.2 = (bf16[1,32,1,16,128]{1,3,4,2,0:T(8,128)(2,1)}, bf16[1,32,1,16,128]{1,3,4,2,0:T(8,128)(2,1)S(1)}, u32[]{:S(2)}, u32[]{:S(2)}) collective-permute-start(bf16[1,32,1,16,128]{1,3,4,2,0:T(8,128)(2,1)} %get-tuple-element.21), channel_id=1, source_target_pairs={{0,1},{1,2},{2,3},{3,4},{4,5},{5,6},{6,7},{7,8},{8,9},{9,10},{10,1... | collective-permute-start | bytes 393224 | tf_op jit(solution)/shard_map/ppermute | solution.py:12
  47.4 4.2 %copy-start.4 = (bf16[1,32,4,16,128]{4,1,3,2,0:T(8,128)(2,1)S(1)}, bf16[1,32,4,16,128]{4,1,3,2,0:T(8,128)(2,1)}, u32[]{:S(2)}) copy-start(bf16[1,32,4,16,128]{4,1,3,2,0:T(8,128)(2,1)} %copy-done.3) | copy-start | bytes 1572868
  50.3 1.4 copy-start.9
  53.0 1.7 copy-start.2
  56.2 1.7 copy-start.7
  59.5 0.8 copy-start.5
  60.4 229.1 %all-reduce.6.cloned.1.call-start = ((), (), s32[]{:S(2)}) async-start(), calls=%async_computation.1 | async-start | bytes 884736 | tf_op jit(solution)/shard_map/psum | solution.py:69
Sparse Core Ops, SparseCore 0:
  60.5 68.6 all-reduce.3
  140.4 148.9 all-reduce.5
